TPU v7x, 128 devices: a whole 4x4x4 slice. The times are simulated.
128 devices in a mesh: wide: 16 (over z_lo, y, core), narrow: 8 (over x, z_hi).
Axes of the slice: x: 4, y: 4, z: 4 (z_hi: 2, z_lo: 2; z = z_hi * 2 + z_lo), core: 2. Of those that a mesh axis runs over, the one named last changes fastest.
Arguments:
- embeddings: bfloat16 [512, 768], P(('wide', 'narrow')), may hold values from -6 to 6
- positives: int32 [512, 16], P(('wide', 'narrow')), may hold values from -1 to 1048575, as said below
- label_weight: bfloat16 [1048576, 768], P(('wide', 'narrow')), may hold values from -0.21875 to 0.21875
- label_bias: float32 [1048576], P(('wide', 'narrow')), may hold values from -8 to -4
Outputs:
- input_grad: float32 [512, 768], P(('wide', 'narrow'))
- weight_grad: bfloat16 [1048576, 768], P(('wide', 'narrow'))
- bias_grad: float32 [1048576], P(('wide', 'narrow'))
Inputs may be any that keep to these rules, and one draw needn't show every extreme that they name: `positives`: each row holds 1 to 16 label ids in its first slots and -1 in the rest; ids may repeat within a row; the first row is full.
All inputs are finite; a program needn't handle non-finite values.
Results may differ from a plain program's by a relative error of at most 0.008.
Values may be sent and summed in bfloat16 or wider, within the bound.
A program may use at most 128 MiB of HBM per device.

v0:
```python
import jax
import jax.numpy as jnp
from jax import lax
from jax.sharding import PartitionSpec as P


def on_device(embeddings, positives, label_weight, label_bias):
    slot_count = positives.shape[1]
    label_rows = label_weight.shape[0]
    narrow_count = lax.axis_size("narrow")
    shard_index = lax.axis_index("wide") * narrow_count + lax.axis_index("narrow")
    offset = shard_index * label_rows
    whole_embed = lax.all_gather(embeddings, ("wide", "narrow"), axis=0, tiled=True)
    whole_ids = lax.all_gather(positives, ("wide", "narrow"), axis=0, tiled=True)
    logits = (
        lax.dot_general(
            whole_embed, label_weight, (((1,), (1,)), ((), ())), preferred_element_type=jnp.float32
        )
        + label_bias[None, :]
    )
    label_index = offset + lax.iota(jnp.int32, label_rows)
    target = jnp.zeros(logits.shape, jnp.float32)
    for column in range(slot_count):
        target = jnp.maximum(
            target, (whole_ids[:, column : column + 1] == label_index[None, :]).astype(jnp.float32)
        )
    grad_full = jax.nn.sigmoid(logits) - target
    grad = grad_full.astype(jnp.bfloat16)
    bias_grad = jnp.sum(grad_full, axis=0)
    weight_grad = lax.dot_general(
        grad, whole_embed, (((0,), (0,)), ((), ())), preferred_element_type=jnp.float32
    ).astype(jnp.bfloat16)
    input_grad = lax.psum_scatter(
        jnp.dot(grad, label_weight, preferred_element_type=jnp.float32),
        ("wide", "narrow"),
        scatter_dimension=0,
        tiled=True,
    )
    return (input_grad, weight_grad, bias_grad)


def solution(mesh):
    in_specs = (
        P(("wide", "narrow"), None),
        P(("wide", "narrow"), None),
        P(("wide", "narrow"), None),
        P(("wide", "narrow")),
    )
    out_specs = (P(("wide", "narrow"), None), P(("wide", "narrow"), None), P(("wide", "narrow")))
    return jax.shard_map(
        on_device, mesh=mesh, in_specs=in_specs, out_specs=out_specs, check_vma=False
    )
```

profile of v0, /device:TPU:1, one launch (start us, length us, event | category | flops | bytes accessed | tf_op | source)
XLA Modules:
  0.0 859.5 jit_solution(17980257496428137566)
XLA Ops:
  7.2 0.0 copy-start.1
  7.2 0.0 all-reduce.3.cloned.1.call-start
  7.2 310.9 %all-gather.1 = s32[128,4,16]{2,1,0:T(4,128)S(1)} all-gather(s32[1,4,16]{2,1,0:T(4,128)} %bitcast.27), channel_id=1, replica_groups=mesh['wide'=16,'narrow'=8] {'wide','narrow'}, dimensions={0}, use_global_device_ids=true | all-gather | bytes 33024 | tf_op jit(solution)/shard_map/all_gather | solution.py:14
  318.1 315.2 %all-gather = bf16[128,4,768]{2,1,0:T(4,128)(2,1)S(1)} all-gather(bf16[1,4,768]{2,1,0:T(4,128)(2,1)} %bitcast.26), channel_id=1, replica_groups=mesh['wide'=16,'narrow'=8] {'wide','narrow'}, dimensions={0}, use_global_device_ids=true | all-gather | bytes 792576 | tf_op jit(solution)/shard_map/all_gather | solution.py:13
  633.3 1.1 reshape.12
  634.3 2.0 fusion.3
  636.3 1.1 copy.39
  637.4 1.1 copy.53
  638.5 1.1 copy.52
  639.5 1.1 copy.51
  640.6 0.1 copy.50
  640.7 0.1 copy.49
  640.8 0.1 copy.48
  641.0 0.1 copy.47
  641.1 0.1 copy.46
  641.2 0.1 copy.45
  641.3 0.1 copy.44
  641.4 0.1 copy.43
  641.6 0.1 copy.42
  641.7 0.1 copy.41
  641.8 0.1 copy.40
  641.9 0.1 copy.54
  642.0 0.0 copy-done.1
  642.0 40.2 %fusion.4 = (f32[8192]{0:T(1024)}, bf16[512,8192]{1,0:T(8,128)(2,1)}) fusion(s32[512]{0:T(512)S(1)} %bitcast.43, s32[512]{0:T(512)S(1)} %bitcast.29, s32[512]{0:T(512)S(1)} %bitcast.30, s32[512]{0:T(512)S(1)} %bitcast.31, s32[512]{0:T(512)S(1)} %bitcast.32, s32[512]{0:T(512)S(1)} %bitcast.33, s32[512]{0:T(512)S(1)} %bitcast.34, s32[512]{0:T(512)S(1)} %bitcast.35, ...), kind=kOutput, calls=%fused_computation.8 | convolution fusion | flops 6673129472 | bytes 21889024 | tf_op jit(solution)/shard_map/dot_general | solution.py:16
  682.2 0.0 copy-start
  682.2 13.6 %fusion.1 = f32[512,768]{1,0:T(8,128)} fusion(bf16[8192,768]{1,0:T(8,128)(2,1)} %param.6, bf16[512,8192]{1,0:T(8,128)(2,1)} %get-tuple-element.20), kind=kOutput, calls=%fused_computation.3 | convolution fusion | flops 6442450944 | bytes 22544384 | tf_op jit(solution)/shard_map/dot_general | solution.py:34
  695.9 0.0 all-reduce.3.cloned.1.call-update
  695.9 0.0 copy-done
  695.9 12.7 %convolution_convert_fusion = bf16[8192,768]{1,0:T(8,128)(2,1)} fusion(bf16[512,768]{1,0:T(8,128)(2,1)S(1)} %copy-done, bf16[512,8192]{1,0:T(8,128)(2,1)} %get-tuple-element.20), kind=kOutput, calls=%fused_computation.1 | convolution fusion | flops 6448742400 | bytes 21757952 | tf_op jit(solution)/shard_map/dot_general | solution.py:30
  708.6 142.8 %all-reduce.3.cloned.1.call-done = f32[512,768]{1,0:T(8,128)} async-done(((f32[512,768]{1,0:T(8,128)}), f32[512,768]{1,0:T(8,128)}) %all-reduce.3.cloned.1.call-update) | async-done | bytes 1572880
  851.3 1.3 constant_dynamic-slice_fusion
  (1 shorter events, 0.0 us)
Async XLA Ops:
  7.2 634.9 %copy-start.1 = (f32[8192]{0:T(1024)S(1)}, f32[8192]{0:T(1024)}, u32[]{:S(2)}) copy-start(f32[8192]{0:T(1024)} %param.7) | copy-start | bytes 98308
  7.2 844.2 %all-reduce.3.cloned.1.call-start = ((), (), s32[]{:S(2)}) async-start(), calls=%async_computation | async-start | bytes 3145728
  682.2 13.7 %copy-start = (bf16[512,768]{1,0:T(8,128)(2,1)S(1)}, bf16[512,768]{1,0:T(8,128)(2,1)}, u32[]{:S(2)}) copy-start(bf16[512,768]{1,0:T(8,128)(2,1)} %reshape.12) | copy-start | bytes 2359300
Sparse Core Ops, SparseCore 0:
  696.0 155.2 all-reduce.2
where the time goes:
time: 860 us
  blocking collectives  626 us (73%)
  waiting for transfers between devices  143 us (17%)
  matrix products  66.5 us (8%)
  between operations  14.1 us (2%)
  local copies, waits for them, and re-layouts  10.1 us (1%)
    all_gather x1, blocking collectives, on_device(): lax.all_gather(embeddings, ('wide', 'narrow'), axis=0, tiled=True)  315 us
    all_gather x1, blocking collectives, on_device(): lax.all_gather(positives, ('wide', 'narrow'), axis=0, tiled=True)  311 us
    unnamed x2, waiting for transfers between devices  143 us
    dot_general x1, matrix products, on_device(): lax.dot_general(whole_embed, label_weight, (((1,), (1,)), ((), ())), pref...  40.2 us
  transfers between devices with their start and end apart: 1, of which 1 were waited for; matrix products, arithmetic and copies ran while one was open for 1% of the time, Pallas kernels for 0%

commit v1 on v0

v1 whole, which is shorter than its diff:
```python
import functools

import jax
import jax.numpy as jnp
from jax import lax
from jax.experimental import pallas as pl
from jax.experimental.pallas import tpu as pltpu
from jax.sharding import PartitionSpec as P

LOG2E = 1.4426950408889634
LANES = 128
ROWS = 32
MESH = pl.DeviceIdType.MESH
BF16 = jnp.bfloat16
F32 = jnp.float32


def aligned(index, size):
    return pl.ds(pl.multiple_of(index, size), size)


def dot_nt(a, b):
    return lax.dot_general(a, b, (((1,), (1,)), ((), ())), preferred_element_type=F32)


def dot_tn(a, b):
    return lax.dot_general(a, b, (((0,), (0,)), ((), ())), preferred_element_type=F32)


def exchange_kernel(
    cfg,
    embed_ref,
    ids_ref,
    weight_hbm,
    bias_ref,
    input_grad_ref,
    bias_grad_ref,
    grad_hbm,
    embed_out,
    part_hbm,
    weight_v,
    grad_v,
    embed_v,
    bias_v,
    sums_v,
    mask_v,
    ids_near,
    ids_far,
    message32,
    message,
    gathered,
    wide32,
    logits_a,
    logits_b,
    grad_a,
    grad_b,
    acc_far,
    acc_own,
    acc_relay,
    outgoing,
    arrived,
    part_v,
    load_sem,
    store_sem,
    gather_sem,
    relay_sem,
    scatter_sem,
):
    labels, depth, tile, part_tile, part_rows, peers, narrow = cfg
    docs = embed_ref.shape[0]
    slots = ids_ref.shape[1]
    half = docs * peers
    lane_tiles = depth // LANES
    wide_index, narrow_index = lax.axis_index("wide"), lax.axis_index("narrow")
    core = lax.rem(wide_index, 2)
    chip = lax.div(wide_index, 2) * narrow + narrow_index
    label_offset = (wide_index * narrow + narrow_index) * labels
    sibling = (wide_index + 1 - 2 * core, narrow_index)

    def device_of(peer, on_core):
        return (2 * lax.div(peer, narrow) + on_core, lax.rem(peer, narrow))

    barrier = pltpu.get_barrier_semaphore()

    @pl.loop(0, peers)
    def _(i):
        pl.semaphore_signal(
            barrier,
            inc=1,
            device_id=device_of(lax.rem(chip + i, peers), 1 - core),
            device_id_type=MESH,
        )

    load = pltpu.make_async_copy(weight_hbm, weight_v, load_sem)
    load.start()

    embed = embed_ref[...].astype(F32)
    for k in range(lane_tiles):
        message32[k * docs : (k + 1) * docs, :] = embed[:, k * LANES : (k + 1) * LANES]
    ids = ids_ref[...]
    zeros = jnp.zeros((docs, LANES - 2 * slots), F32)
    high = jnp.right_shift(ids, 13).astype(F32)
    middle = (jnp.right_shift(ids, 8) & 31).astype(F32)
    low = (ids & 255).astype(F32)
    base = lane_tiles * docs
    message32[base : base + docs, :] = jnp.concatenate([high, middle, zeros], axis=1)
    message32[base + docs : base + 2 * docs, :] = jnp.concatenate([low, low, zeros], axis=1)
    message[...] = message32[...].astype(BF16)

    pl.semaphore_wait(barrier, peers)

    @pl.loop(0, peers)
    def _(i):
        pltpu.make_async_remote_copy(
            src_ref=message,
            dst_ref=gathered.at[aligned(chip * ROWS, ROWS)],
            send_sem=gather_sem.at[0],
            recv_sem=gather_sem.at[1],
            device_id=device_of(lax.rem(chip + i, peers), 1 - core),
            device_id_type=MESH,
        ).start()

    @pl.loop(0, labels // (8 * LANES))
    def _(i):
        rows = bias_ref[aligned(i * 8, 8), :] * (-LOG2E)
        for j in range(8):
            spread = jnp.broadcast_to(rows[j : j + 1, :], (LANES, LANES)).T
            bias_v[aligned(i * (8 * LANES) + j * LANES, LANES), :] = spread

    pltpu.make_async_copy(gathered, gathered, gather_sem.at[1]).wait()

    for i in range(8):
        step = peers * ROWS // 8
        wide32[i * step : (i + 1) * step, :] = gathered[i * step : (i + 1) * step, :].astype(F32)

    def picked(row):
        return wide32[pl.ds(row, peers, stride=ROWS), :]

    for k in range(lane_tiles):
        for r in range(docs):
            embed_v[r * peers : (r + 1) * peers, k * LANES : (k + 1) * LANES] = picked(
                k * docs + r
            ).astype(BF16)
    for pair in range(docs // 2):
        first = base + 2 * pair
        upper = jnp.concatenate([picked(first), picked(first + 1)], axis=0).T
        lower = jnp.concatenate([picked(first + docs), picked(first + docs + 1)], axis=0).T
        whole = upper[:slots] * 8192.0 + upper[slots : 2 * slots] * 256.0 + lower[:slots]
        ids_near[:, pair * LANES : (pair + 1) * LANES] = whole.astype(jnp.int32)

    relays = [
        pltpu.make_async_remote_copy(
            src_ref=source,
            dst_ref=target,
            send_sem=relay_sem.at[2 * n],
            recv_sem=relay_sem.at[2 * n + 1],
            device_id=sibling,
            device_id_type=MESH,
        )
        for n, (source, target) in enumerate(
            [
                (embed_v.at[0:half], embed_v.at[half : 2 * half]),
                (ids_near, ids_far),
                (acc_far, acc_relay),
            ]
        )
    ]
    relays[0].start()
    relays[1].start()

    groups = labels // 32

    def fill_mask(ids_v, chunk):
        local = ids_v[...] - label_offset
        local = jnp.where((local >= 0) & (local < labels), local, -1)
        group = jnp.right_shift(local, 5)
        bit = jnp.left_shift(jnp.ones_like(local), local & 31)

        @pl.loop(0, groups // 32)
        def _(i):
            index = lax.broadcasted_iota(jnp.int32, (32, half), 0) + i * 32
            words = jnp.zeros((32, half), jnp.int32)
            for j in range(slots):
                words = words | jnp.where(group[j : j + 1, :] == index, bit[j : j + 1, :], 0)
            mask_v[aligned(i * 32, 32), :] = words

    def run_chunk(chunk, acc):
        acc[...] = jnp.zeros_like(acc)
        columns = slice(chunk * half, (chunk + 1) * half)

        def logits(i, out):
            out[...] = dot_nt(weight_v[aligned(i * tile, tile), :], embed_v[columns, :])

        def gradient(i, logit, out):
            bits = jnp.left_shift(1, lax.broadcasted_iota(jnp.int32, (32, LANES), 0))
            words = mask_v[aligned(i * (tile // 32), tile // 32), :]
            for g in range(tile // 32):
                rows = aligned(i * tile + g * 32, 32)
                bias = bias_v[rows, :]
                total = None
                for h in range(half // LANES):
                    lanes = slice(h * LANES, (h + 1) * LANES)
                    x = logit[g * 32 : (g + 1) * 32, lanes]
                    sigmoid = pltpu.reciprocal(
                        1.0 + jnp.exp2(x * (-LOG2E) + bias), approx=True
                    )
                    hit = (words[g : g + 1, lanes] & bits) != 0
                    full = sigmoid - jnp.where(hit, 1.0, 0.0)
                    total = full if total is None else total + full
                    rounded = full.astype(BF16)
                    out[g * 32 : (g + 1) * 32, lanes] = rounded
                    grad_v[rows, chunk * half + h * LANES : chunk * half + (h + 1) * LANES] = (
                        rounded
                    )
                if chunk == 0:
                    sums_v[rows, :] = total
                else:
                    sums_v[rows, :] += total

        def back(i, grad):
            acc[...] += dot_tn(grad[...], weight_v[aligned(i * tile, tile), :])

        tiles = labels // tile
        logits(0, logits_a)
        logits(1, logits_b)
        gradient(0, logits_a, grad_a)

        @pl.loop(1, tiles - 1, step=2)
        def _(i):
            back(i - 1, grad_a)
            logits(i + 1, logits_a)
            gradient(i, logits_b, grad_b)
            back(i, grad_b)
            logits(i + 2, logits_b)
            gradient(i + 1, logits_a, grad_a)

        back(tiles - 2, grad_a)
        gradient(tiles - 1, logits_b, grad_b)
        back(tiles - 1, grad_b)

    fill_mask(ids_near, 0)
    load.wait()
    run_chunk(0, acc_far)
    relays[2].start()
    relays[0].wait()
    relays[1].wait()
    fill_mask(ids_far, 1)
    run_chunk(1, acc_own)

    grad_store = pltpu.make_async_copy(
        grad_v.at[pl.ds(part_rows, labels - part_rows)], grad_hbm, store_sem.at[0]
    )
    grad_store.start()
    embed_out[...] = embed_v[...]

    relays[2].wait()
    for k in range(lane_tiles):
        lanes = slice(k * LANES, (k + 1) * LANES)
        for r in range(docs):
            rows = slice(r * peers, (r + 1) * peers)
            wide32[pl.ds(k * docs + r, peers, stride=ROWS), :] = (
                acc_own[rows, lanes] + acc_relay[rows, lanes]
            )
    for i in range(8):
        step = peers * ROWS // 8
        outgoing[i * step : (i + 1) * step, :] = wide32[i * step : (i + 1) * step, :].astype(BF16)

    @pl.loop(1, peers)
    def _(i):
        peer = lax.rem(chip + i, peers)
        pltpu.make_async_remote_copy(
            src_ref=outgoing.at[aligned(peer * ROWS, ROWS)],
            dst_ref=arrived.at[aligned(chip * ROWS, ROWS)],
            send_sem=scatter_sem.at[0],
            recv_sem=scatter_sem.at[1],
            device_id=device_of(peer, core),
            device_id_type=MESH,
        ).start()

    arrived[aligned(chip * ROWS, ROWS), :] = outgoing[aligned(chip * ROWS, ROWS), :]

    @pl.loop(0, part_rows // part_tile)
    def _(i):
        rows = aligned(i * part_tile, part_tile)
        part_v[rows, :] = jnp.dot(
            grad_v[rows, :], embed_v[...], preferred_element_type=F32
        ).astype(BF16)
        pltpu.make_async_copy(part_v.at[rows], part_hbm.at[rows], store_sem.at[1]).start()

    @pl.loop(0, labels // (8 * LANES))
    def _(i):
        rows = [
            jnp.sum(sums_v[aligned(i * (8 * LANES) + j * LANES, LANES), :].T, axis=0, keepdims=True)
            for j in range(8)
        ]
        bias_grad_ref[aligned(i * 8, 8), :] = jnp.concatenate(rows, axis=0)

    others = (peers - 1) * ROWS
    pltpu.make_async_copy(
        arrived.at[0:others], arrived.at[0:others], scatter_sem.at[1]
    ).wait()
    group = 8

    def add(i, total):
        block = arrived[aligned(i * (group * ROWS), group * ROWS), :].astype(F32)
        for j in range(group):
            total = total + block[j * ROWS : (j + 1) * ROWS, :]
        return total

    total = lax.fori_loop(0, peers // group, add, jnp.zeros((ROWS, LANES), F32))
    for k in range(lane_tiles):
        input_grad_ref[:, k * LANES : (k + 1) * LANES] = total[k * docs : (k + 1) * docs, :]

    pltpu.make_async_copy(
        outgoing.at[0:others], outgoing.at[0:others], scatter_sem.at[0]
    ).wait()
    pltpu.make_async_copy(gathered, gathered, gather_sem.at[0]).wait()
    grad_store.wait()
    pltpu.make_async_copy(part_v, part_hbm, store_sem.at[1]).wait()


def finish_kernel(
    cfg,
    grad_hbm,
    embed_ref,
    part_hbm,
    input_grad_in,
    bias_grad_in,
    input_grad_ref,
    weight_grad_hbm,
    bias_grad_ref,
    grad_v,
    out_v,
    load_sems,
    store_sem,
    part_sem,
):
    part_rows, tile = cfg
    rest = grad_hbm.shape[0]
    tiles = rest // tile

    def load(i):
        rows = aligned(i * tile, tile)
        return pltpu.make_async_copy(grad_hbm.at[rows], grad_v.at[rows], load_sems.at[i])

    for i in range(tiles):
        load(i).start()
    part = pltpu.make_async_copy(part_hbm, weight_grad_hbm.at[pl.ds(0, part_rows)], part_sem)
    part.start()
    input_grad_ref[...] = input_grad_in[...]
    bias_grad_ref[...] = bias_grad_in[...]

    @pl.loop(0, tiles)
    def _(i):
        load(i).wait()
        rows = aligned(i * tile, tile)
        out_v[rows, :] = jnp.dot(
            grad_v[rows, :], embed_ref[...], preferred_element_type=F32
        ).astype(BF16)
        pltpu.make_async_copy(
            out_v.at[rows],
            weight_grad_hbm.at[aligned(part_rows + i * tile, tile)],
            store_sem,
        ).start()

    pltpu.make_async_copy(
        out_v, weight_grad_hbm.at[pl.ds(part_rows, rest)], store_sem
    ).wait()
    part.wait()


def on_device(embeddings, positives, label_weight, label_bias):
    docs, depth = embeddings.shape
    slots = positives.shape[1]
    labels = label_weight.shape[0]
    narrow = lax.axis_size("narrow")
    peers = lax.axis_size("wide") * narrow // 2
    half = docs * peers
    part_rows = labels // 2
    rest = labels - part_rows
    tile, part_tile, rest_tile = 1024, 2048, 1024
    vmem = pl.BlockSpec(memory_space=pltpu.VMEM)
    hbm = pl.BlockSpec(memory_space=pl.ANY)
    shape = jax.ShapeDtypeStruct

    flops = 2 * 2 * labels * 2 * half * depth
    input_grad, bias_grad, grad_rest, embed_all, part = pl.pallas_call(
        functools.partial(
            exchange_kernel, (labels, depth, tile, part_tile, part_rows, peers, narrow)
        ),
        out_shape=[
            shape((docs, depth), F32),
            shape((labels // LANES, LANES), F32),
            shape((rest, 2 * half), BF16),
            shape((2 * half, depth), BF16),
            shape((part_rows, depth), BF16),
        ],
        in_specs=[vmem, vmem, hbm, vmem],
        out_specs=[vmem, vmem, hbm, vmem, hbm],
        scratch_shapes=[
            pltpu.VMEM((labels, depth), BF16),
            pltpu.VMEM((labels, 2 * half), BF16),
            pltpu.VMEM((2 * half, depth), BF16),
            pltpu.VMEM((labels, LANES), F32),
            pltpu.VMEM((labels, LANES), F32),
            pltpu.VMEM((labels // 32, half), jnp.int32),
            pltpu.VMEM((slots, half), jnp.int32),
            pltpu.VMEM((slots, half), jnp.int32),
            pltpu.VMEM((ROWS, LANES), F32),
            pltpu.VMEM((ROWS, LANES), BF16),
            pltpu.VMEM((peers * ROWS, LANES), BF16),
            pltpu.VMEM((peers * ROWS, LANES), F32),
            pltpu.VMEM((tile, half), F32),
            pltpu.VMEM((tile, half), F32),
            pltpu.VMEM((tile, half), BF16),
            pltpu.VMEM((tile, half), BF16),
            pltpu.VMEM((half, depth), F32),
            pltpu.VMEM((half, depth), F32),
            pltpu.VMEM((half, depth), F32),
            pltpu.VMEM((peers * ROWS, LANES), BF16),
            pltpu.VMEM((peers * ROWS, LANES), BF16),
            pltpu.VMEM((part_rows, depth), BF16),
            pltpu.SemaphoreType.DMA,
            pltpu.SemaphoreType.DMA((2,)),
            pltpu.SemaphoreType.DMA((2,)),
            pltpu.SemaphoreType.DMA((6,)),
            pltpu.SemaphoreType.DMA((2,)),
        ],
        compiler_params=pltpu.CompilerParams(
            collective_id=0, has_side_effects=True, vmem_limit_bytes=60 * 2**20
        ),
        cost_estimate=pl.CostEstimate(
            flops=flops, bytes_accessed=labels * depth * 3, transcendentals=0
        ),
        name="exchange",
    )(embeddings, positives, label_weight, label_bias.reshape(labels // LANES, LANES))

    input_grad, weight_grad, bias_grad = pl.pallas_call(
        functools.partial(finish_kernel, (part_rows, rest_tile)),
        out_shape=[
            shape((docs, depth), F32),
            shape((labels, depth), BF16),
            shape((labels // LANES, LANES), F32),
        ],
        in_specs=[hbm, vmem, hbm, vmem, vmem],
        out_specs=[vmem, hbm, vmem],
        scratch_shapes=[
            pltpu.VMEM((rest, 2 * half), BF16),
            pltpu.VMEM((rest, depth), BF16),
            pltpu.SemaphoreType.DMA((rest // rest_tile,)),
            pltpu.SemaphoreType.DMA,
            pltpu.SemaphoreType.DMA,
        ],
        compiler_params=pltpu.CompilerParams(vmem_limit_bytes=48 * 2**20),
        cost_estimate=pl.CostEstimate(
            flops=flops // 4, bytes_accessed=labels * depth * 4, transcendentals=0
        ),
        name="finish",
    )(grad_rest, embed_all, part, input_grad, bias_grad)
    return input_grad, weight_grad, bias_grad.reshape(labels)


def solution(mesh):
    in_specs = (
        P(("wide", "narrow"), None),
        P(("wide", "narrow"), None),
        P(("wide", "narrow"), None),
        P(("wide", "narrow")),
    )
    out_specs = (P(("wide", "narrow"), None), P(("wide", "narrow"), None), P(("wide", "narrow")))
    return jax.shard_map(
        on_device, mesh=mesh, in_specs=in_specs, out_specs=out_specs, check_vma=False
    )
```

time: 860 us -> 249 us (0.29)
  blocking collectives: 626 us -> 0 us
  Pallas kernels: 0 us -> 243 us
  waiting for transfers between devices: 143 us -> 0 us
  matrix products: 66.5 us -> 0 us
  between operations: 14.1 us -> 0.65 us
    all_gather x2 -> x0, blocking collectives: 626 us -> none  [the longest x1 315 us: on_device(): lax.all_gather(embeddings, ('wide', 'narrow'), axis=0, tiled=True)]
    pallas_call x0 -> x2, Pallas kernels: none -> 243 us  [the longest x1 193 us: on_device(): pl.pallas_call(functools.partial(finish_kernel, (part_rows, rest_tile)),...]
    unnamed x2 -> x0, waiting for transfers between devices: 143 us -> none
    dot_general x3 -> x0, matrix products: 66.5 us -> none  [the longest x1 40.2 us: on_device(): lax.dot_general(whole_embed, label_weight, (((1,), (1,)), ((), ())), pref...]
  transfers between devices with their start and end apart: 1 -> 0, of which waited for: 1 -> 0; matrix products, arithmetic and copies ran while one was open for 1% -> 0% of each run, Pallas kernels for 0% -> 0%
where the time goes in v1:
time: 249 us
  Pallas kernels  243 us (98%)
  local copies, waits for them, and re-layouts  4.78 us (2%)
    pallas_call x1, Pallas kernels, on_device(): pl.pallas_call(functools.partial(finish_kernel, (part_rows, rest_tile)),...  193 us
    pallas_call x1, Pallas kernels, on_device(): pl.pallas_call(functools.partial(exchange_kernel, (labels, depth, tile, p...  50.7 us

profile of v1, /device:TPU:1, one launch (start us, length us, event | category | flops | bytes accessed | tf_op | source)
XLA Modules:
  0.0 248.8 jit_solution(17199521321513604523)
XLA Ops:
  0.6 50.7 %exchange.1 = (f32[4,768]{1,0:T(4,128)}, f32[64,128]{1,0:T(8,128)}, bf16[4096,512]{1,0:T(8,128)(2,1)}, bf16[512,768]{1,0:T(8,128)(2,1)}, bf16[4096,768]{1,0:T(8,128)(2,1)}) custom-call(bf16[4,768]{1,0:T(4,128)(2,1)} %embed_ref.1, s32[4,16]{1,0:T(4,128)} %ids_ref.1, bf16[8192,768]{1,0:T(8,128)(2,1)} %weight_hbm.1, f32[64,128]{1,0:T(8,128)} %bitcast.2), custom_call_target="tpu_custom_call" | custom-call | flops 12884901888 | bytes 18874368 | tf_op jit(solution)/shard_map/exchange/pallas_call | solution.py:387
  51.3 0.0 copy-start
  51.3 2.2 copy-done
  53.5 0.0 copy-start.1
  53.5 1.1 copy-done.1
  54.7 0.0 copy-start.2
  54.7 0.8 copy-done.2
  55.4 0.0 copy-start.3
  55.4 0.7 copy-done.3
  56.1 192.6 %finish.1 = (f32[4,768]{1,0:T(4,128)}, bf16[8192,768]{1,0:T(8,128)(2,1)}, f32[64,128]{1,0:T(8,128)}) custom-call(bf16[4096,512]{1,0:T(8,128)(2,1)S(1)} %copy-done, bf16[512,768]{1,0:T(8,128)(2,1)S(1)} %copy-done.1, bf16[4096,768]{1,0:T(8,128)(2,1)} %get-tuple-element.13.part_hbm, f32[4,768]{1,0:T(4,128)S(1)} %copy-done.3, f32[64,128]{1,0:T(8,128)S(1)} %copy-done.2), custom_call_target="tpu_custom_call" | custom-call | flops 3221225472 | bytes 25165824 | tf_op jit(solution)/shard_map/finish/pallas_call | solution.py:438
Async XLA Ops:
  51.3 2.2 copy-start
  53.5 1.1 copy-start.1
  54.7 0.8 copy-start.2
  55.4 0.7 copy-start.3

commit v2 on v1

v2 whole, which is shorter than its diff:
```python
import functools

import jax
import jax.numpy as jnp
from jax import lax
from jax.experimental import pallas as pl
from jax.experimental.pallas import tpu as pltpu
from jax.sharding import PartitionSpec as P

LOG2E = 1.4426950408889634
LANES = 128
PART = 3
TILE = 1024
PIECES = 1
MESH = pl.DeviceIdType.MESH
BF16 = jnp.bfloat16
F32 = jnp.float32


def aligned(index, size):
    return pl.ds(pl.multiple_of(index, size), size)


def dot_nt(a, b):
    return lax.dot_general(a, b, (((1,), (1,)), ((), ())), preferred_element_type=F32)


def dot_tn(a, b):
    return lax.dot_general(a, b, (((0,), (0,)), ((), ())), preferred_element_type=F32)


def exchange_kernel(
    cfg,
    embed_ref,
    ids_ref,
    weight_hbm,
    bias_ref,
    input_grad_ref,
    bias_grad_ref,
    grad_v,
    embed_out,
    part_v,
    weight_v,
    embed_v,
    bias_v,
    sums_v,
    mask_v,
    ids_near,
    ids_far,
    message32,
    message,
    ids_message,
    gathered,
    ids_gathered,
    wide32,
    ids_wide32,
    logits_a,
    logits_b,
    grad_a,
    grad_b,
    acc_far,
    acc_own,
    acc_relay,
    outgoing,
    arrived,
    load_sem,
    gather_sem,
    ids_sem,
    relay_sem,
    scatter_sem,
):
    labels, depth, tile, part_tile, part_rows, peers, narrow = cfg
    docs = embed_ref.shape[0]
    slots = ids_ref.shape[1]
    half = docs * peers
    lane_tiles = depth // LANES
    wide_index, narrow_index = lax.axis_index("wide"), lax.axis_index("narrow")
    core = lax.rem(wide_index, 2)
    chip = lax.div(wide_index, 2) * narrow + narrow_index
    label_offset = (wide_index * narrow + narrow_index) * labels
    sibling = (wide_index + 1 - 2 * core, narrow_index)

    def device_of(peer, on_core):
        return (2 * lax.div(peer, narrow) + on_core, lax.rem(peer, narrow))

    barrier = pltpu.get_barrier_semaphore()

    @pl.loop(0, peers)
    def _(i):
        pl.semaphore_signal(
            barrier,
            inc=1,
            device_id=device_of(lax.rem(chip + i, peers), 1 - core),
            device_id_type=MESH,
        )

    load = pltpu.make_async_copy(weight_hbm, weight_v, load_sem)
    load.start()

    embed = embed_ref[...].astype(F32)
    for k in range(lane_tiles):
        message32[k * docs : (k + 1) * docs, :] = embed[:, k * LANES : (k + 1) * LANES]
    ids = ids_ref[...]
    zeros = jnp.zeros((docs, LANES - 2 * slots), F32)
    high = jnp.right_shift(ids, 13).astype(F32)
    middle = (jnp.right_shift(ids, 8) & 31).astype(F32)
    low = (ids & 255).astype(F32)
    message[...] = message32[...].astype(BF16)
    ids_rows = [
        jnp.concatenate([high, middle, zeros], axis=1),
        jnp.concatenate([low, low, zeros], axis=1),
    ]
    ids_message[...] = jnp.concatenate(ids_rows, axis=0).astype(BF16)

    pl.semaphore_wait(barrier, peers)

    for source, target, sems in [
        (message, gathered, gather_sem),
        (ids_message, ids_gathered, ids_sem),
    ]:

        @pl.loop(0, peers)
        def _(i):
            pltpu.make_async_remote_copy(
                src_ref=source,
                dst_ref=target.at[chip],
                send_sem=sems.at[0],
                recv_sem=sems.at[1],
                device_id=device_of(lax.rem(chip + i, peers), 1 - core),
                device_id_type=MESH,
            ).start()

    @pl.loop(0, labels // (8 * LANES))
    def _(i):
        rows = bias_ref[aligned(i * 8, 8), :] * (-LOG2E)
        for j in range(8):
            spread = jnp.broadcast_to(rows[j : j + 1, :], (LANES, LANES)).T
            bias_v[aligned(i * (8 * LANES) + j * LANES, LANES), :] = spread

    pltpu.make_async_copy(gathered, gathered, gather_sem.at[1]).wait()

    rows_of = lane_tiles * docs
    blocks = peers // 8
    for i in range(8):
        wide32[i * blocks * rows_of : (i + 1) * blocks * rows_of, :] = (
            gathered[i * blocks : (i + 1) * blocks].astype(F32).reshape(blocks * rows_of, LANES)
        )

    for k in range(lane_tiles):
        for r in range(docs):
            embed_v[r * peers : (r + 1) * peers, k * LANES : (k + 1) * LANES] = wide32[
                pl.ds(k * docs + r, peers, stride=rows_of), :
            ].astype(BF16)

    relays = [
        pltpu.make_async_remote_copy(
            src_ref=source,
            dst_ref=target,
            send_sem=relay_sem.at[2 * n],
            recv_sem=relay_sem.at[2 * n + 1],
            device_id=sibling,
            device_id_type=MESH,
        )
        for n, (source, target) in enumerate(
            [
                (embed_v.at[0:half], embed_v.at[half : 2 * half]),
                (ids_near, ids_far),
                (acc_far, acc_relay),
            ]
        )
    ]
    relays[0].start()

    def decode_ids():
        pltpu.make_async_copy(ids_gathered, ids_gathered, ids_sem.at[1]).wait()
        ids_wide32[...] = ids_gathered[...].astype(F32).reshape(peers * 2 * docs, LANES)

        def picked(row):
            return ids_wide32[pl.ds(row, peers, stride=2 * docs), :]

        for pair in range(docs // 2):
            first = 2 * pair
            upper = jnp.concatenate([picked(first), picked(first + 1)], axis=0).T
            lower = jnp.concatenate([picked(first + docs), picked(first + docs + 1)], axis=0).T
            whole = upper[:slots] * 8192.0 + upper[slots : 2 * slots] * 256.0 + lower[:slots]
            ids_near[:, pair * LANES : (pair + 1) * LANES] = whole.astype(jnp.int32)
        relays[1].start()

    groups = labels // 32

    def fill_mask(ids_v):
        local = ids_v[...] - label_offset
        local = jnp.where((local >= 0) & (local < labels), local, -1)
        group = jnp.right_shift(local, 5)
        bit = jnp.left_shift(jnp.ones_like(local), local & 31)

        @pl.loop(0, groups // 32)
        def _(i):
            index = lax.broadcasted_iota(jnp.int32, (32, half), 0) + i * 32
            words = jnp.zeros((32, half), jnp.int32)
            for j in range(slots):
                words = words | jnp.where(group[j : j + 1, :] == index, bit[j : j + 1, :], 0)
            mask_v[aligned(i * 32, 32), :] = words

    def run_chunk(chunk, acc, prepare):
        acc[...] = jnp.zeros_like(acc)
        columns = slice(chunk * half, (chunk + 1) * half)

        def logits(i, out):
            out[...] = dot_nt(weight_v[aligned(i * tile, tile), :], embed_v[columns, :])

        def gradient(i, logit, out):
            bits = jnp.left_shift(1, lax.broadcasted_iota(jnp.int32, (32, LANES), 0))
            words = mask_v[aligned(i * (tile // 32), tile // 32), :]
            for g in range(tile // 32):
                rows = aligned(i * tile + g * 32, 32)
                bias = bias_v[rows, :]
                total = None
                for h in range(half // LANES):
                    lanes = slice(h * LANES, (h + 1) * LANES)
                    x = logit[g * 32 : (g + 1) * 32, lanes]
                    sigmoid = pltpu.reciprocal(
                        1.0 + jnp.exp2(x * (-LOG2E) + bias), approx=True
                    )
                    hit = (words[g : g + 1, lanes] & bits) != 0
                    full = sigmoid - jnp.where(hit, 1.0, 0.0)
                    total = full if total is None else total + full
                    rounded = full.astype(BF16)
                    out[g * 32 : (g + 1) * 32, lanes] = rounded
                    grad_v[rows, chunk * half + h * LANES : chunk * half + (h + 1) * LANES] = (
                        rounded
                    )
                if chunk == 0:
                    sums_v[rows, :] = total
                else:
                    sums_v[rows, :] += total

        def back(i, grad):
            acc[...] += dot_tn(grad[...], weight_v[aligned(i * tile, tile), :])

        tiles = labels // tile
        logits(0, logits_a)
        logits(1, logits_b)
        prepare()
        gradient(0, logits_a, grad_a)

        @pl.loop(1, tiles - 1, step=2)
        def _(i):
            back(i - 1, grad_a)
            logits(i + 1, logits_a)
            gradient(i, logits_b, grad_b)
            back(i, grad_b)
            logits(i + 2, logits_b)
            gradient(i + 1, logits_a, grad_a)

        back(tiles - 2, grad_a)
        gradient(tiles - 1, logits_b, grad_b)
        back(tiles - 1, grad_b)

    def prepare_near():
        decode_ids()
        fill_mask(ids_near)

    def prepare_far():
        relays[1].wait()
        fill_mask(ids_far)

    load.wait()
    run_chunk(0, acc_far, prepare_near)
    relays[2].start()
    relays[0].wait()
    run_chunk(1, acc_own, prepare_far)
    embed_out[...] = embed_v[...]

    relays[2].wait()
    for k in range(lane_tiles):
        lanes = slice(k * LANES, (k + 1) * LANES)
        for r in range(docs):
            rows = slice(r * peers, (r + 1) * peers)
            wide32[pl.ds(k * docs + r, peers, stride=rows_of), :] = (
                acc_own[rows, lanes] + acc_relay[rows, lanes]
            )
    for i in range(8):
        outgoing[i * blocks : (i + 1) * blocks] = (
            wide32[i * blocks * rows_of : (i + 1) * blocks * rows_of, :]
            .reshape(blocks, rows_of, LANES)
            .astype(BF16)
        )

    @pl.loop(1, peers)
    def _(step):
        peer = lax.rem(chip + step, peers)
        pltpu.make_async_remote_copy(
            src_ref=outgoing.at[peer],
            dst_ref=arrived.at[chip],
            send_sem=scatter_sem.at[0],
            recv_sem=scatter_sem.at[1],
            device_id=device_of(peer, core),
            device_id_type=MESH,
        ).start()

    arrived[chip] = outgoing[chip]

    @pl.loop(0, part_rows // part_tile)
    def _(i):
        rows = aligned(i * part_tile, part_tile)
        part_v[rows, :] = jnp.dot(
            grad_v[rows, :], embed_v[...], preferred_element_type=F32
        ).astype(BF16)

    @pl.loop(0, labels // (8 * LANES))
    def _(i):
        rows = [
            jnp.sum(sums_v[aligned(i * (8 * LANES) + j * LANES, LANES), :].T, axis=0, keepdims=True)
            for j in range(8)
        ]
        bias_grad_ref[aligned(i * 8, 8), :] = jnp.concatenate(rows, axis=0)

    others = arrived.at[0 : peers - 1]
    pltpu.make_async_copy(others, others, scatter_sem.at[1]).wait()

    def add(i, total):
        return total + jnp.sum(arrived[pl.ds(i * blocks, blocks)].astype(F32), axis=0)

    total = lax.fori_loop(0, 8, add, jnp.zeros((rows_of, LANES), F32))
    for k in range(lane_tiles):
        input_grad_ref[:, k * LANES : (k + 1) * LANES] = total[k * docs : (k + 1) * docs, :]

    others = outgoing.at[0 : peers - 1]
    pltpu.make_async_copy(others, others, scatter_sem.at[0]).wait()
    pltpu.make_async_copy(gathered, gathered, gather_sem.at[0]).wait()
    pltpu.make_async_copy(ids_gathered, ids_gathered, ids_sem.at[0]).wait()


def finish_kernel(
    cfg,
    grad_v,
    embed_v,
    part_v,
    input_grad_in,
    bias_grad_in,
    input_grad_ref,
    weight_grad_hbm,
    bias_grad_ref,
    out_v,
    store_sem,
):
    part_rows, tile = cfg
    labels = weight_grad_hbm.shape[0]
    rest = labels - part_rows
    piece = part_rows // PIECES
    for i in range(PIECES):
        rows = pl.ds(i * piece, piece)
        pltpu.make_async_copy(part_v.at[rows], weight_grad_hbm.at[rows], store_sem.at[0]).start()
    input_grad_ref[...] = input_grad_in[...]
    bias_grad_ref[...] = bias_grad_in[...]

    @pl.loop(0, rest // tile)
    def _(i):
        rows = aligned(i * tile, tile)
        out_v[rows, :] = jnp.dot(
            grad_v[aligned(part_rows + i * tile, tile), :],
            embed_v[...],
            preferred_element_type=F32,
        ).astype(BF16)
        pltpu.make_async_copy(
            out_v.at[rows],
            weight_grad_hbm.at[aligned(part_rows + i * tile, tile)],
            store_sem.at[1],
        ).start()

    pltpu.make_async_copy(
        out_v, weight_grad_hbm.at[pl.ds(part_rows, rest)], store_sem.at[1]
    ).wait()
    pltpu.make_async_copy(
        part_v, weight_grad_hbm.at[pl.ds(0, part_rows)], store_sem.at[0]
    ).wait()


def on_device(embeddings, positives, label_weight, label_bias):
    docs, depth = embeddings.shape
    slots = positives.shape[1]
    labels = label_weight.shape[0]
    narrow = lax.axis_size("narrow")
    peers = lax.axis_size("wide") * narrow // 2
    half = docs * peers
    part_rows = labels * PART // 4
    rest = labels - part_rows
    rows = depth // LANES * docs
    tile, part_tile, rest_tile = TILE, 2048, 1024
    vmem = pl.BlockSpec(memory_space=pltpu.VMEM)
    hbm = pl.BlockSpec(memory_space=pl.ANY)
    shape = jax.ShapeDtypeStruct

    flops = 2 * 2 * labels * 2 * half * depth
    input_grad, bias_grad, grad_all, embed_all, part = pl.pallas_call(
        functools.partial(
            exchange_kernel, (labels, depth, tile, part_tile, part_rows, peers, narrow)
        ),
        out_shape=[
            pltpu.VMEM((docs, depth), F32),
            pltpu.VMEM((labels // LANES, LANES), F32),
            pltpu.VMEM((labels, 2 * half), BF16),
            pltpu.VMEM((2 * half, depth), BF16),
            pltpu.VMEM((part_rows, depth), BF16),
        ],
        in_specs=[vmem, vmem, hbm, vmem],
        out_specs=[vmem] * 5,
        scratch_shapes=[
            pltpu.VMEM((labels, depth), BF16),
            pltpu.VMEM((2 * half, depth), BF16),
            pltpu.VMEM((labels, LANES), F32),
            pltpu.VMEM((labels, LANES), F32),
            pltpu.VMEM((labels // 32, half), jnp.int32),
            pltpu.VMEM((slots, half), jnp.int32),
            pltpu.VMEM((slots, half), jnp.int32),
            pltpu.VMEM((rows, LANES), F32),
            pltpu.VMEM((rows, LANES), BF16),
            pltpu.VMEM((2 * docs, LANES), BF16),
            pltpu.VMEM((peers, rows, LANES), BF16),
            pltpu.VMEM((peers, 2 * docs, LANES), BF16),
            pltpu.VMEM((peers * rows, LANES), F32),
            pltpu.VMEM((peers * 2 * docs, LANES), F32),
            pltpu.VMEM((tile, half), F32),
            pltpu.VMEM((tile, half), F32),
            pltpu.VMEM((tile, half), BF16),
            pltpu.VMEM((tile, half), BF16),
            pltpu.VMEM((half, depth), F32),
            pltpu.VMEM((half, depth), F32),
            pltpu.VMEM((half, depth), F32),
            pltpu.VMEM((peers, rows, LANES), BF16),
            pltpu.VMEM((peers, rows, LANES), BF16),
            pltpu.SemaphoreType.DMA,
            pltpu.SemaphoreType.DMA((2,)),
            pltpu.SemaphoreType.DMA((2,)),
            pltpu.SemaphoreType.DMA((6,)),
            pltpu.SemaphoreType.DMA((2,)),
        ],
        compiler_params=pltpu.CompilerParams(
            collective_id=0, has_side_effects=True, vmem_limit_bytes=44 * 2**20
        ),
        cost_estimate=pl.CostEstimate(
            flops=flops, bytes_accessed=labels * depth * 3, transcendentals=0
        ),
        name="exchange",
    )(embeddings, positives, label_weight, label_bias.reshape(labels // LANES, LANES))

    input_grad, weight_grad, bias_grad = pl.pallas_call(
        functools.partial(finish_kernel, (part_rows, rest_tile)),
        out_shape=[
            shape((docs, depth), F32),
            shape((labels, depth), BF16),
            shape((labels // LANES, LANES), F32),
        ],
        in_specs=[vmem] * 5,
        out_specs=[vmem, hbm, vmem],
        scratch_shapes=[
            pltpu.VMEM((rest, depth), BF16),
            pltpu.SemaphoreType.DMA((2,)),
        ],
        compiler_params=pltpu.CompilerParams(vmem_limit_bytes=8 * 2**20),
        cost_estimate=pl.CostEstimate(
            flops=flops // 4, bytes_accessed=labels * depth * 4, transcendentals=0
        ),
        name="finish",
    )(
        pltpu.with_memory_space_constraint(grad_all, pltpu.VMEM),
        pltpu.with_memory_space_constraint(embed_all, pltpu.VMEM),
        pltpu.with_memory_space_constraint(part, pltpu.VMEM),
        pltpu.with_memory_space_constraint(input_grad, pltpu.VMEM),
        pltpu.with_memory_space_constraint(bias_grad, pltpu.VMEM),
    )
    return input_grad, weight_grad, bias_grad.reshape(labels)


def solution(mesh):
    in_specs = (
        P(("wide", "narrow"), None),
        P(("wide", "narrow"), None),
        P(("wide", "narrow"), None),
        P(("wide", "narrow")),
    )
    out_specs = (P(("wide", "narrow"), None), P(("wide", "narrow"), None), P(("wide", "narrow")))
    return jax.shard_map(
        on_device, mesh=mesh, in_specs=in_specs, out_specs=out_specs, check_vma=False
    )
```

time: 249 us -> 53.7 us (0.22)
  Pallas kernels: 243 us -> 52.8 us
  local copies, waits for them, and re-layouts: 4.78 us -> 0 us
    pallas_call x1, Pallas kernels: 193 us -> 5.36 us  [on_device(): pl.pallas_call(functools.partial(finish_kernel, (part_rows, rest_tile)),...]
    unnamed x8 -> x0, local copies, waits for them, and re-layouts: 4.78 us -> none
    pallas_call x1, Pallas kernels: 50.7 us -> 47.5 us  [on_device(): pl.pallas_call(functools.partial(exchange_kernel, (labels, depth, tile, p...]
where the time goes in v2:
time: 53.7 us; the launch traced here: 53.5 us
  Pallas kernels  52.8 us (98%)
  between operations  0.64 us (1%)
    pallas_call x1, Pallas kernels, on_device(): pl.pallas_call(functools.partial(exchange_kernel, (labels, depth, tile, p...  47.5 us
    pallas_call x1, Pallas kernels, on_device(): pl.pallas_call(functools.partial(finish_kernel, (part_rows, rest_tile)),...  5.36 us

profile of v2, /device:TPU:1, one launch (start us, length us, event | category | flops | bytes accessed | tf_op | source)
XLA Modules:
  0.0 53.5 jit_solution(3532690700950505530)
XLA Ops:
  0.6 47.5 %exchange.1 = (f32[4,768]{1,0:T(4,128)S(1)}, f32[64,128]{1,0:T(8,128)S(1)}, bf16[8192,512]{1,0:T(8,128)(2,1)S(1)}, bf16[512,768]{1,0:T(8,128)(2,1)S(1)}, bf16[6144,768]{1,0:T(8,128)(2,1)S(1)}) custom-call(bf16[4,768]{1,0:T(4,128)(2,1)} %embed_ref.1, s32[4,16]{1,0:T(4,128)} %ids_ref.1, bf16[8192,768]{1,0:T(8,128)(2,1)} %weight_hbm.1, f32[64,128]{1,0:T(8,128)} %bitcast.2), custom_call_target="tpu_custom_call" | custom-call | flops 12884901888 | bytes 18874368 | tf_op jit(solution)/shard_map/exchange/pallas_call | solution.py:396
  48.1 5.4 %finish.1 = (f32[4,768]{1,0:T(4,128)}, bf16[8192,768]{1,0:T(8,128)(2,1)}, f32[64,128]{1,0:T(8,128)}) custom-call(bf16[8192,512]{1,0:T(8,128)(2,1)S(1)} %get-tuple-element.11.grad_v, bf16[512,768]{1,0:T(8,128)(2,1)S(1)} %get-tuple-element.12.embed_v, bf16[6144,768]{1,0:T(8,128)(2,1)S(1)} %get-tuple-element.13.part_v, ...), custom_call_target="tpu_custom_call" | custom-call | flops 3221225472 | bytes 25165824 | tf_op jit(solution)/shard_map/finish/pallas_call | solution.py:448

commit v3 on v2

v3 whole, which is shorter than its diff:
```python
import functools
import itertools

import jax
import jax.numpy as jnp
from jax import lax
from jax.experimental import pallas as pl
from jax.experimental.pallas import tpu as pltpu
from jax.sharding import PartitionSpec as P

LOG2E = 1.4426950408889634
LANES = 128
TILE = 1024
PART = 3
MESH = pl.DeviceIdType.MESH
BF16 = jnp.bfloat16
F32 = jnp.float32


def aligned(index, size):
    return pl.ds(pl.multiple_of(index, size), size)


def dot_nt(a, b):
    return lax.dot_general(a, b, (((1,), (1,)), ((), ())), preferred_element_type=F32)


def dot_tn(a, b):
    return lax.dot_general(a, b, (((0,), (0,)), ((), ())), preferred_element_type=F32)


def exchange_kernel(
    cfg,
    embed_ref,
    ids_ref,
    weight_hbm,
    bias_ref,
    input_grad_ref,
    bias_grad_ref,
    grad_out,
    embed_out,
    part_v,
    weight_v,
    grad_v,
    embed_v,
    bias_v,
    sums_v,
    mask_v,
    ids_near,
    ids_far,
    message32,
    message,
    ids_message,
    gathered,
    ids_gathered,
    wide32,
    ids_wide32,
    logits_a,
    logits_b,
    grad_a,
    grad_b,
    acc_far,
    acc_own,
    acc_relay,
    outgoing,
    arrived,
    load_sem,
    gather_sem,
    ids_sem,
    relay_sem,
    scatter_sem,
    hand_sem,
):
    labels, depth, tile, part_tile, peers, narrow = cfg
    docs = embed_ref.shape[0]
    slots = ids_ref.shape[1]
    half = docs * peers
    lane_tiles = depth // LANES
    wide_index, narrow_index = lax.axis_index("wide"), lax.axis_index("narrow")
    core = lax.rem(wide_index, 2)
    chip = lax.div(wide_index, 2) * narrow + narrow_index
    label_offset = (wide_index * narrow + narrow_index) * labels
    sibling = (wide_index + 1 - 2 * core, narrow_index)

    y, x = lax.rem(lax.div(wide_index, 2), 4), lax.div(narrow_index, 2)
    z_low, z_high = lax.div(wide_index, 8), lax.rem(narrow_index, 2)
    z = z_high * 2 + z_low
    reach = (0, 1, 2, 1)
    steps = itertools.product(range(4), range(4), range(4))
    steps = sorted(steps, key=lambda step: -sum(reach[part] for part in step))
    places = []
    for part in range(4):
        turned = lax.rem(z + part, 4)
        places.append(
            (
                2 * lax.rem(x + part, 4),
                2 * lax.rem(y + part, 4),
                8 * lax.rem(turned, 2),
                lax.div(turned, 2),
            )
        )

    def device_at(step, on_core):
        along_x, along_y, along_z = (places[part] for part in step)
        return (along_z[2] + along_y[1] + on_core, along_x[0] + along_z[3])

    def device_of(peer, on_core):
        return (2 * lax.div(peer, narrow) + on_core, lax.rem(peer, narrow))

    barrier = pltpu.get_barrier_semaphore()

    @pl.loop(0, peers)
    def _(i):
        pl.semaphore_signal(
            barrier,
            inc=1,
            device_id=device_of(lax.rem(chip + i, peers), 1 - core),
            device_id_type=MESH,
        )

    load = pltpu.make_async_copy(weight_hbm, weight_v, load_sem)
    load.start()

    embed = embed_ref[...].astype(F32)
    for k in range(lane_tiles):
        message32[k * docs : (k + 1) * docs, :] = embed[:, k * LANES : (k + 1) * LANES]
    ids = ids_ref[...]
    zeros = jnp.zeros((docs, LANES - 2 * slots), F32)
    high = jnp.right_shift(ids, 13).astype(F32)
    middle = (jnp.right_shift(ids, 8) & 31).astype(F32)
    low = (ids & 255).astype(F32)
    message[...] = message32[...].astype(BF16)
    ids_rows = [
        jnp.concatenate([high, middle, zeros], axis=1),
        jnp.concatenate([low, low, zeros], axis=1),
    ]
    ids_message[...] = jnp.concatenate(ids_rows, axis=0).astype(BF16)

    pl.semaphore_wait(barrier, peers)

    def give(source, target, sems, device):
        pltpu.make_async_remote_copy(
            src_ref=source,
            dst_ref=target.at[chip],
            send_sem=sems.at[0],
            recv_sem=sems.at[1],
            device_id=device,
            device_id_type=MESH,
        ).start()

    for step in steps:
        give(message, gathered, gather_sem, device_at(step, 1 - core))

    @pl.loop(0, peers)
    def _(i):
        peer = lax.rem(chip + i, peers)
        give(ids_message, ids_gathered, ids_sem, device_of(peer, 1 - core))

    @pl.loop(0, labels // (8 * LANES))
    def _(i):
        rows = bias_ref[aligned(i * 8, 8), :] * (-LOG2E)
        for j in range(8):
            spread = jnp.broadcast_to(rows[j : j + 1, :], (LANES, LANES)).T
            bias_v[aligned(i * (8 * LANES) + j * LANES, LANES), :] = spread

    pltpu.make_async_copy(gathered, gathered, gather_sem.at[1]).wait()

    rows_of = lane_tiles * docs
    blocks = peers // 8
    for i in range(8):
        wide32[i * blocks * rows_of : (i + 1) * blocks * rows_of, :] = (
            gathered[i * blocks : (i + 1) * blocks].astype(F32).reshape(blocks * rows_of, LANES)
        )

    for k in range(lane_tiles):
        for r in range(docs):
            embed_v[r * peers : (r + 1) * peers, k * LANES : (k + 1) * LANES] = wide32[
                pl.ds(k * docs + r, peers, stride=rows_of), :
            ].astype(BF16)

    relays = [
        pltpu.make_async_remote_copy(
            src_ref=source,
            dst_ref=target,
            send_sem=relay_sem.at[2 * n],
            recv_sem=relay_sem.at[2 * n + 1],
            device_id=sibling,
            device_id_type=MESH,
        )
        for n, (source, target) in enumerate(
            [
                (embed_v.at[0:half], embed_v.at[half : 2 * half]),
                (ids_near, ids_far),
                (acc_far, acc_relay),
            ]
        )
    ]
    relays[0].start()

    def decode_ids():
        pltpu.make_async_copy(ids_gathered, ids_gathered, ids_sem.at[1]).wait()
        ids_wide32[...] = ids_gathered[...].astype(F32).reshape(peers * 2 * docs, LANES)

        def picked(row):
            return ids_wide32[pl.ds(row, peers, stride=2 * docs), :]

        for pair in range(docs // 2):
            first = 2 * pair
            upper = jnp.concatenate([picked(first), picked(first + 1)], axis=0).T
            lower = jnp.concatenate([picked(first + docs), picked(first + docs + 1)], axis=0).T
            whole = upper[:slots] * 8192.0 + upper[slots : 2 * slots] * 256.0 + lower[:slots]
            ids_near[:, pair * LANES : (pair + 1) * LANES] = whole.astype(jnp.int32)
        relays[1].start()

    def fill_mask(ids_v, chunk):
        local = ids_v[...] - label_offset
        local = jnp.where((local >= 0) & (local < labels), local, -1)
        group = jnp.right_shift(local, 5)
        bit = jnp.left_shift(jnp.ones_like(local), local & 31)

        for i in range(labels // 1024):
            index = lax.broadcasted_iota(jnp.int32, (32, half), 0) + i * 32
            words = jnp.zeros((32, half), jnp.int32)
            for j in range(slots):
                words = words | jnp.where(group[j : j + 1, :] == index, bit[j : j + 1, :], 0)
            mask_v[chunk, i * 32 : (i + 1) * 32, :] = words

    def logits(chunk, i, out):
        out[...] = dot_nt(
            weight_v[aligned(i * tile, tile), :], embed_v[chunk * half : (chunk + 1) * half, :]
        )

    def gradient(chunk, i, logit, out):
        bits = jnp.left_shift(1, lax.broadcasted_iota(jnp.int32, (32, LANES), 0))
        words = mask_v[chunk, aligned(i * (tile // 32), tile // 32), :]
        for g in range(tile // 32):
            rows = aligned(i * tile + g * 32, 32)
            bias = bias_v[rows, :]
            total = None
            for h in range(half // LANES):
                lanes = slice(h * LANES, (h + 1) * LANES)
                x = logit[g * 32 : (g + 1) * 32, lanes]
                sigmoid = pltpu.reciprocal(1.0 + jnp.exp2(x * (-LOG2E) + bias), approx=True)
                hit = (words[g : g + 1, lanes] & bits) != 0
                full = sigmoid - jnp.where(hit, 1.0, 0.0)
                total = full if total is None else total + full
                rounded = full.astype(BF16)
                out[g * 32 : (g + 1) * 32, lanes] = rounded
                start = chunk * half + h * LANES
                grad_v[rows, start : start + LANES] = rounded
            sums_v[chunk, rows, :] = total

    def back(i, grad, acc):
        acc[...] += dot_tn(grad[...], weight_v[aligned(i * tile, tile), :])

    tiles = labels // tile
    acc_far[...] = jnp.zeros_like(acc_far)
    acc_own[...] = jnp.zeros_like(acc_own)
    load.wait()
    logits(0, 0, logits_a)
    logits(0, 1, logits_b)
    decode_ids()
    fill_mask(ids_near, 0)
    gradient(0, 0, logits_a, grad_a)

    def steps_of(chunk, first, last, acc):
        @pl.loop(first, last, step=2)
        def _(i):
            back(i - 1, grad_a, acc)
            logits(chunk, i + 1, logits_a)
            gradient(chunk, i, logits_b, grad_b)
            back(i, grad_b, acc)
            logits(chunk, i + 2, logits_b)
            gradient(chunk, i + 1, logits_a, grad_a)

    steps_of(0, 1, tiles - 1, acc_far)
    relays[0].wait()
    relays[1].wait()
    fill_mask(ids_far, 1)
    back(tiles - 2, grad_a, acc_far)
    logits(1, 0, logits_a)
    gradient(0, tiles - 1, logits_b, grad_b)
    back(tiles - 1, grad_b, acc_far)
    logits(1, 1, logits_b)
    gradient(1, 0, logits_a, grad_a)
    relays[2].start()
    steps_of(1, 1, tiles - 1, acc_own)
    back(tiles - 2, grad_a, acc_own)
    gradient(1, tiles - 1, logits_b, grad_b)
    back(tiles - 1, grad_b, acc_own)

    done = part_v.shape[0]
    hands = [
        pltpu.make_async_copy(grad_v.at[pl.ds(done, labels - done)], grad_out, hand_sem.at[0]),
        pltpu.make_async_copy(embed_v, embed_out, hand_sem.at[1]),
    ]
    for hand in hands:
        hand.start()

    relays[2].wait()
    for k in range(lane_tiles):
        lanes = slice(k * LANES, (k + 1) * LANES)
        for r in range(docs):
            rows = slice(r * peers, (r + 1) * peers)
            wide32[pl.ds(k * docs + r, peers, stride=rows_of), :] = (
                acc_own[rows, lanes] + acc_relay[rows, lanes]
            )
    for i in range(8):
        outgoing[i * blocks : (i + 1) * blocks] = (
            wide32[i * blocks * rows_of : (i + 1) * blocks * rows_of, :]
            .reshape(blocks, rows_of, LANES)
            .astype(BF16)
        )

    for step in steps[:-1]:
        wide_to, narrow_to = device_at(step, core)
        peer = lax.div(wide_to, 2) * narrow + narrow_to
        give(outgoing.at[peer], arrived, scatter_sem, (wide_to, narrow_to))

    arrived[chip] = outgoing[chip]

    @pl.loop(0, done // part_tile)
    def _(i):
        rows = aligned(i * part_tile, part_tile)
        part_v[rows, :] = jnp.dot(
            grad_v[rows, :], embed_v[...], preferred_element_type=F32
        ).astype(BF16)

    def summed(rows):
        return jnp.sum((sums_v[0, rows, :] + sums_v[1, rows, :]).T, axis=0, keepdims=True)

    @pl.loop(0, labels // (8 * LANES))
    def _(i):
        rows = [
            summed(aligned(i * (8 * LANES) + j * LANES, LANES))
            for j in range(8)
        ]
        bias_grad_ref[aligned(i * 8, 8), :] = jnp.concatenate(rows, axis=0)

    others = arrived.at[0 : peers - 1]
    pltpu.make_async_copy(others, others, scatter_sem.at[1]).wait()

    def add(i, total):
        return total + jnp.sum(arrived[pl.ds(i * blocks, blocks)].astype(F32), axis=0)

    total = lax.fori_loop(0, 8, add, jnp.zeros((rows_of, LANES), F32))
    for k in range(lane_tiles):
        input_grad_ref[:, k * LANES : (k + 1) * LANES] = total[k * docs : (k + 1) * docs, :]

    others = outgoing.at[0 : peers - 1]
    pltpu.make_async_copy(others, others, scatter_sem.at[0]).wait()
    for hand in hands:
        hand.wait()
    pltpu.make_async_copy(gathered, gathered, gather_sem.at[0]).wait()
    pltpu.make_async_copy(ids_gathered, ids_gathered, ids_sem.at[0]).wait()


def finish_kernel(
    tile,
    grad_v,
    embed_v,
    part_v,
    input_grad_in,
    bias_grad_in,
    input_grad_ref,
    weight_grad_hbm,
    bias_grad_ref,
    rest_v,
    part_sem,
    rest_sem,
):
    done, rest = part_v.shape[0], rest_v.shape[0]
    part = pltpu.make_async_copy(part_v, weight_grad_hbm.at[pl.ds(0, done)], part_sem)
    part.start()
    input_grad_ref[...] = input_grad_in[...]
    bias_grad_ref[...] = bias_grad_in[...]

    @pl.loop(0, rest // tile)
    def _(i):
        rows = aligned(i * tile, tile)
        rest_v[rows, :] = jnp.dot(
            grad_v[rows, :], embed_v[...], preferred_element_type=F32
        ).astype(BF16)
        pltpu.make_async_copy(
            rest_v.at[rows], weight_grad_hbm.at[aligned(done + i * tile, tile)], rest_sem
        ).start()

    pltpu.make_async_copy(rest_v, weight_grad_hbm.at[pl.ds(done, rest)], rest_sem).wait()
    part.wait()


def on_device(embeddings, positives, label_weight, label_bias):
    docs, depth = embeddings.shape
    slots = positives.shape[1]
    labels = label_weight.shape[0]
    narrow = lax.axis_size("narrow")
    peers = lax.axis_size("wide") * narrow // 2
    half = docs * peers
    rows = depth // LANES * docs
    tile, part_tile = TILE, 2048
    part_rows = labels * PART // 4
    vmem = pl.BlockSpec(memory_space=pltpu.VMEM)
    hbm = pl.BlockSpec(memory_space=pl.ANY)
    shape = jax.ShapeDtypeStruct

    flops = 3 * 2 * labels * 2 * half * depth
    input_grad, bias_grad, grad_rest, embed_all, part = pl.pallas_call(
        functools.partial(
            exchange_kernel, (labels, depth, tile, part_tile, peers, narrow)
        ),
        out_shape=[
            pltpu.VMEM((docs, depth), F32),
            pltpu.VMEM((labels // LANES, LANES), F32),
            pltpu.VMEM((labels - part_rows, 2 * half), BF16),
            pltpu.VMEM((2 * half, depth), BF16),
            pltpu.VMEM((part_rows, depth), BF16),
        ],
        in_specs=[vmem, vmem, hbm, vmem],
        out_specs=[vmem] * 5,
        scratch_shapes=[
            pltpu.VMEM((labels, depth), BF16),
            pltpu.VMEM((labels, 2 * half), BF16),
            pltpu.VMEM((2 * half, depth), BF16),
            pltpu.VMEM((labels, LANES), F32),
            pltpu.VMEM((2, labels, LANES), F32),
            pltpu.VMEM((2, labels // 32, half), jnp.int32),
            pltpu.VMEM((slots, half), jnp.int32),
            pltpu.VMEM((slots, half), jnp.int32),
            pltpu.VMEM((rows, LANES), F32),
            pltpu.VMEM((rows, LANES), BF16),
            pltpu.VMEM((2 * docs, LANES), BF16),
            pltpu.VMEM((peers, rows, LANES), BF16),
            pltpu.VMEM((peers, 2 * docs, LANES), BF16),
            pltpu.VMEM((peers * rows, LANES), F32),
            pltpu.VMEM((peers * 2 * docs, LANES), F32),
            pltpu.VMEM((tile, half), F32),
            pltpu.VMEM((tile, half), F32),
            pltpu.VMEM((tile, half), BF16),
            pltpu.VMEM((tile, half), BF16),
            pltpu.VMEM((half, depth), F32),
            pltpu.VMEM((half, depth), F32),
            pltpu.VMEM((half, depth), F32),
            pltpu.VMEM((peers, rows, LANES), BF16),
            pltpu.VMEM((peers, rows, LANES), BF16),
            pltpu.SemaphoreType.DMA,
            pltpu.SemaphoreType.DMA((2,)),
            pltpu.SemaphoreType.DMA((2,)),
            pltpu.SemaphoreType.DMA((6,)),
            pltpu.SemaphoreType.DMA((2,)),
            pltpu.SemaphoreType.DMA((2,)),
        ],
        compiler_params=pltpu.CompilerParams(
            collective_id=0, has_side_effects=True, vmem_limit_bytes=46 * 2**20
        ),
        cost_estimate=pl.CostEstimate(
            flops=flops, bytes_accessed=labels * depth * 3, transcendentals=0
        ),
        name="exchange",
    )(embeddings, positives, label_weight, label_bias.reshape(labels // LANES, LANES))

    handed = [
        pltpu.with_memory_space_constraint(array, pltpu.VMEM)
        for array in (grad_rest, embed_all, part, input_grad, bias_grad)
    ]
    input_grad, weight_grad, bias_grad = pl.pallas_call(
        functools.partial(finish_kernel, 1024),
        out_shape=[
            shape((docs, depth), F32),
            shape((labels, depth), BF16),
            shape((labels // LANES, LANES), F32),
        ],
        in_specs=[vmem] * 5,
        out_specs=[vmem, hbm, vmem],
        scratch_shapes=[
            pltpu.VMEM((labels - part_rows, depth), BF16),
            pltpu.SemaphoreType.DMA,
            pltpu.SemaphoreType.DMA,
        ],
        compiler_params=pltpu.CompilerParams(vmem_limit_bytes=16 * 2**20),
        cost_estimate=pl.CostEstimate(
            flops=flops // 12, bytes_accessed=labels * depth * 2, transcendentals=0
        ),
        name="finish",
    )(*handed)
    return input_grad, weight_grad, bias_grad.reshape(labels)


def solution(mesh):
    in_specs = (
        P(("wide", "narrow"), None),
        P(("wide", "narrow"), None),
        P(("wide", "narrow"), None),
        P(("wide", "narrow")),
    )
    out_specs = (P(("wide", "narrow"), None), P(("wide", "narrow"), None), P(("wide", "narrow")))
    return jax.shard_map(
        on_device, mesh=mesh, in_specs=in_specs, out_specs=out_specs, check_vma=False
    )
```

time: 53.7 us -> 51.6 us (0.961)
  Pallas kernels: 52.8 us -> 50.8 us
    pallas_call x1, Pallas kernels: 47.5 us -> 45.4 us  [on_device(): pl.pallas_call(functools.partial(exchange_kernel, (labels, depth, tile, p...]
where the time goes in v3:
time: 51.6 us; the launch traced here: 51.4 us
  Pallas kernels  50.8 us (98%)
  between operations  0.64 us (1%)
    pallas_call x1, Pallas kernels, on_device(): pl.pallas_call(functools.partial(exchange_kernel, (labels, depth, tile, p...  45.4 us
    pallas_call x1, Pallas kernels, on_device(): pl.pallas_call(functools.partial(finish_kernel, 1024), out_shape=[shape((...  5.36 us

profile of v3, /device:TPU:1, one launch (start us, length us, event | category | flops | bytes accessed | tf_op | source)
XLA Modules:
  0.0 51.4 jit_solution(5087211824584958698)
XLA Ops:
  0.6 45.4 %exchange.1 = (f32[4,768]{1,0:T(4,128)S(1)}, f32[64,128]{1,0:T(8,128)S(1)}, bf16[2048,512]{1,0:T(8,128)(2,1)S(1)}, bf16[512,768]{1,0:T(8,128)(2,1)S(1)}, bf16[6144,768]{1,0:T(8,128)(2,1)S(1)}) custom-call(bf16[4,768]{1,0:T(4,128)(2,1)} %embed_ref.1, s32[4,16]{1,0:T(4,128)} %ids_ref.1, bf16[8192,768]{1,0:T(8,128)(2,1)} %weight_hbm.1, f32[64,128]{1,0:T(8,128)} %bitcast.2), custom_call_target="tpu_custom_call" | custom-call | flops 19327352832 | bytes 18874368 | tf_op jit(solution)/shard_map/exchange/pallas_call | solution.py:407
  46.0 5.4 %finish.1 = (f32[4,768]{1,0:T(4,128)}, bf16[8192,768]{1,0:T(8,128)(2,1)}, f32[64,128]{1,0:T(8,128)}) custom-call(bf16[2048,512]{1,0:T(8,128)(2,1)S(1)} %get-tuple-element.11.grad_v, bf16[512,768]{1,0:T(8,128)(2,1)S(1)} %get-tuple-element.12.embed_v, bf16[6144,768]{1,0:T(8,128)(2,1)S(1)} %get-tuple-element.13.part_v, ...), custom_call_target="tpu_custom_call" | custom-call | flops 1610612736 | bytes 12582912 | tf_op jit(solution)/shard_map/finish/pallas_call | solution.py:465

commit v4 on v3

--- a/solution.py
+++ b/solution.py
@@ -11,6 +11,7 @@
 LOG2E = 1.4426950408889634
 LANES = 128
 TILE = 1024
+UNROLL = 2
 PART = 3
 MESH = pl.DeviceIdType.MESH
 BF16 = jnp.bfloat16
@@ -109,13 +110,9 @@
 
     barrier = pltpu.get_barrier_semaphore()
 
-    @pl.loop(0, peers)
-    def _(i):
+    for place in steps:
         pl.semaphore_signal(
-            barrier,
-            inc=1,
-            device_id=device_of(lax.rem(chip + i, peers), 1 - core),
-            device_id_type=MESH,
+            barrier, inc=1, device_id=device_at(place, 1 - core), device_id_type=MESH
         )
 
     load = pltpu.make_async_copy(weight_hbm, weight_v, load_sem)
@@ -148,8 +145,8 @@
             device_id_type=MESH,
         ).start()
 
-    for step in steps:
-        give(message, gathered, gather_sem, device_at(step, 1 - core))
+    for place in steps:
+        give(message, gathered, gather_sem, device_at(place, 1 - core))
 
     @pl.loop(0, peers)
     def _(i):
@@ -257,37 +254,38 @@
     acc_far[...] = jnp.zeros_like(acc_far)
     acc_own[...] = jnp.zeros_like(acc_own)
     load.wait()
+    logits_of, grads_of, accs = (logits_a, logits_b), (grad_a, grad_b), (acc_far, acc_own)
+
+    def step(now, last=None, following=None, odd=0):
+        if last is not None:
+            back(last[1], grads_of[1 - odd], accs[last[0]])
+        if following is not None:
+            logits(*following, logits_of[1 - odd])
+        gradient(*now, logits_of[odd], grads_of[odd])
+
+    def steps_of(chunk, first, last):
+        @pl.loop(first, last, step=UNROLL)
+        def _(i):
+            for j in range(UNROLL):
+                step((chunk, i + j), (chunk, i + j - 1), (chunk, i + j + 1), (1 + j) % 2)
+
     logits(0, 0, logits_a)
     logits(0, 1, logits_b)
     decode_ids()
     fill_mask(ids_near, 0)
-    gradient(0, 0, logits_a, grad_a)
-
-    def steps_of(chunk, first, last, acc):
-        @pl.loop(first, last, step=2)
-        def _(i):
-            back(i - 1, grad_a, acc)
-            logits(chunk, i + 1, logits_a)
-            gradient(chunk, i, logits_b, grad_b)
-            back(i, grad_b, acc)
-            logits(chunk, i + 2, logits_b)
-            gradient(chunk, i + 1, logits_a, grad_a)
-
-    steps_of(0, 1, tiles - 1, acc_far)
+    step((0, 0))
+    steps_of(0, 1, tiles - UNROLL + 1)
     relays[0].wait()
     relays[1].wait()
     fill_mask(ids_far, 1)
-    back(tiles - 2, grad_a, acc_far)
-    logits(1, 0, logits_a)
-    gradient(0, tiles - 1, logits_b, grad_b)
-    back(tiles - 1, grad_b, acc_far)
-    logits(1, 1, logits_b)
-    gradient(1, 0, logits_a, grad_a)
+    order = [(0, i) for i in range(tiles - UNROLL, tiles)] + [(1, 0), (1, 1)]
+    for j in range(1, len(order) - 1):
+        step(order[j], order[j - 1], order[j + 1], j % 2)
     relays[2].start()
-    steps_of(1, 1, tiles - 1, acc_own)
-    back(tiles - 2, grad_a, acc_own)
-    gradient(1, tiles - 1, logits_b, grad_b)
-    back(tiles - 1, grad_b, acc_own)
+    steps_of(1, 1, tiles - UNROLL + 1)
+    for i in range(tiles - UNROLL + 1, tiles):
+        step((1, i), (1, i - 1), (1, i + 1) if i + 1 < tiles else None, i % 2)
+    back(tiles - 1, grads_of[(tiles - 1) % 2], acc_own)
 
     done = part_v.shape[0]
     hands = [
@@ -312,8 +310,8 @@
             .astype(BF16)
         )
 
-    for step in steps[:-1]:
-        wide_to, narrow_to = device_at(step, core)
+    for place in steps[:-1]:
+        wide_to, narrow_to = device_at(place, core)
         peer = lax.div(wide_to, 2) * narrow + narrow_to
         give(outgoing.at[peer], arrived, scatter_sem, (wide_to, narrow_to))
 

time: 51.6 us -> 51.1 us (level)
  no operation moved by 1% of the time
where the time goes in v4:
time: 51.1 us; the launch traced here: 50.9 us
  Pallas kernels  50.3 us (98%)
  between operations  0.64 us (1%)
    pallas_call x1, Pallas kernels, on_device(): pl.pallas_call(functools.partial(exchange_kernel, (labels, depth, tile, p...  44.9 us
    pallas_call x1, Pallas kernels, on_device(): pl.pallas_call(functools.partial(finish_kernel, 1024), out_shape=[shape((...  5.36 us

profile of v4, /device:TPU:1, one launch (start us, length us, event | category | flops | bytes accessed | tf_op | source)
XLA Modules:
  0.0 50.9 jit_solution(11829039593980013877)
XLA Ops:
  0.6 44.9 %exchange.1 = (f32[4,768]{1,0:T(4,128)S(1)}, f32[64,128]{1,0:T(8,128)S(1)}, bf16[2048,512]{1,0:T(8,128)(2,1)S(1)}, bf16[512,768]{1,0:T(8,128)(2,1)S(1)}, bf16[6144,768]{1,0:T(8,128)(2,1)S(1)}) custom-call(bf16[4,768]{1,0:T(4,128)(2,1)} %embed_ref.1, s32[4,16]{1,0:T(4,128)} %ids_ref.1, bf16[8192,768]{1,0:T(8,128)(2,1)} %weight_hbm.1, f32[64,128]{1,0:T(8,128)} %bitcast.2), custom_call_target="tpu_custom_call" | custom-call | flops 19327352832 | bytes 18874368 | tf_op jit(solution)/shard_map/exchange/pallas_call | solution.py:405
  45.6 5.4 %finish.1 = (f32[4,768]{1,0:T(4,128)}, bf16[8192,768]{1,0:T(8,128)(2,1)}, f32[64,128]{1,0:T(8,128)}) custom-call(bf16[2048,512]{1,0:T(8,128)(2,1)S(1)} %get-tuple-element.11.grad_v, bf16[512,768]{1,0:T(8,128)(2,1)S(1)} %get-tuple-element.12.embed_v, bf16[6144,768]{1,0:T(8,128)(2,1)S(1)} %get-tuple-element.13.part_v, ...), custom_call_target="tpu_custom_call" | custom-call | flops 1610612736 | bytes 12582912 | tf_op jit(solution)/shard_map/finish/pallas_call | solution.py:463

commit v5 on v4

--- a/solution.py
+++ b/solution.py
@@ -292,9 +292,6 @@
         pltpu.make_async_copy(grad_v.at[pl.ds(done, labels - done)], grad_out, hand_sem.at[0]),
         pltpu.make_async_copy(embed_v, embed_out, hand_sem.at[1]),
     ]
-    for hand in hands:
-        hand.start()
-
     relays[2].wait()
     for k in range(lane_tiles):
         lanes = slice(k * LANES, (k + 1) * LANES)
@@ -316,6 +313,8 @@
         give(outgoing.at[peer], arrived, scatter_sem, (wide_to, narrow_to))
 
     arrived[chip] = outgoing[chip]
+    for hand in hands:
+        hand.start()
 
     @pl.loop(0, done // part_tile)
     def _(i):
@@ -395,7 +394,7 @@
     peers = lax.axis_size("wide") * narrow // 2
     half = docs * peers
     rows = depth // LANES * docs
-    tile, part_tile = TILE, 2048
+    tile, part_tile = TILE, 3072
     part_rows = labels * PART // 4
     vmem = pl.BlockSpec(memory_space=pltpu.VMEM)
     hbm = pl.BlockSpec(memory_space=pl.ANY)

time: 51.1 us -> 51 us (level)
  no operation moved by 1% of the time
where the time goes in v5:
time: 51 us; the launch traced here: 50.8 us
  Pallas kernels  50.1 us (98%)
  between operations  0.64 us (1%)
    pallas_call x1, Pallas kernels, on_device(): pl.pallas_call(functools.partial(exchange_kernel, (labels, depth, tile, p...  44.8 us
    pallas_call x1, Pallas kernels, on_device(): pl.pallas_call(functools.partial(finish_kernel, 1024), out_shape=[shape((...  5.36 us

profile of v5, /device:TPU:1, one launch (start us, length us, event | category | flops | bytes accessed | tf_op | source)
XLA Modules:
  0.0 50.8 jit_solution(9977724083885006834)
XLA Ops:
  0.6 44.8 %exchange.1 = (f32[4,768]{1,0:T(4,128)S(1)}, f32[64,128]{1,0:T(8,128)S(1)}, bf16[2048,512]{1,0:T(8,128)(2,1)S(1)}, bf16[512,768]{1,0:T(8,128)(2,1)S(1)}, bf16[6144,768]{1,0:T(8,128)(2,1)S(1)}) custom-call(bf16[4,768]{1,0:T(4,128)(2,1)} %embed_ref.1, s32[4,16]{1,0:T(4,128)} %ids_ref.1, bf16[8192,768]{1,0:T(8,128)(2,1)} %weight_hbm.1, f32[64,128]{1,0:T(8,128)} %bitcast.2), custom_call_target="tpu_custom_call" | custom-call | flops 19327352832 | bytes 18874368 | tf_op jit(solution)/shard_map/exchange/pallas_call | solution.py:404
  45.4 5.4 %finish.1 = (f32[4,768]{1,0:T(4,128)}, bf16[8192,768]{1,0:T(8,128)(2,1)}, f32[64,128]{1,0:T(8,128)}) custom-call(bf16[2048,512]{1,0:T(8,128)(2,1)S(1)} %get-tuple-element.11.grad_v, bf16[512,768]{1,0:T(8,128)(2,1)S(1)} %get-tuple-element.12.embed_v, bf16[6144,768]{1,0:T(8,128)(2,1)S(1)} %get-tuple-element.13.part_v, ...), custom_call_target="tpu_custom_call" | custom-call | flops 1610612736 | bytes 12582912 | tf_op jit(solution)/shard_map/finish/pallas_call | solution.py:462
